TPU v7x, 32 devices: a whole 2x2x4 slice. The times are simulated.
32 devices in a mesh: tile: 16 (over z, x, core), lev: 2 (over y).
Axes of the slice: x: 2, y: 2, z: 4, core: 2. Of those that a mesh axis runs over, the one named last changes fastest.
Arguments:
- tracers: bfloat16 [8, 8, 256, 128], P(None, 'lev', 'tile'), may hold values from -6 to 6
- wind_field: bfloat16 [3, 8, 256, 128], P(None, 'lev', 'tile'), may hold values from -5 to 5
- regions: int32 [4, 256, 2], P(None, 'tile'), may hold values from 0 to 15, as said below
- stencil_base: int32 [4, 2, 256, 128], P(None, None, 'tile'), may hold values from 0 to 28, as said below
- far_start: int32 [4, 16, 2], replicated, may hold values from 0 to 15, as said below
Outputs:
- tracers_new: bfloat16 [8, 8, 256, 128], P(None, 'lev', 'tile')
- displacement: float32 [3, 8, 256, 128], P(None, 'lev', 'tile')
Inputs may be any that keep to these rules, and one draw needn't show every extreme that they name: For an arrival block of band r, regions[k, j, 0] lies in r - 2 to r + 1 and in 0 to 14, and regions[k, j, 1] in 0 to 15. Every column that band r's patches at section k take from band r - 2 lies in the cyclic run of 8 columns from far_start[k, r - 2, 0], and every column taken from band r + 2 in the run from far_start[k, r + 2, 1]. stencil_base[k, 0] is at most 28 and stencil_base[k, 1] at most 12.
All inputs are finite; a program needn't handle non-finite values.
Results may differ from a plain program's by a relative error of at most 0.001.
Values may be sent and summed in bfloat16 or wider, within the bound.
A program may use at most 64 MiB of HBM per device.

v0:
```python
import functools

import jax
import jax.numpy as jnp
from jax import lax
from jax.experimental import pallas as pl
from jax.experimental.pallas import tpu as pltpu
from jax.sharding import PartitionSpec as P

ITERS = 3
BW = 16
BH = 8
MESH = pl.DeviceIdType.MESH


def lagrange_cubic(position):
    return [
        -(position - 1.0) * (position - 2.0) * (position - 3.0) / 6.0,
        position * (position - 2.0) * (position - 3.0) / 2.0,
        -position * (position - 1.0) * (position - 3.0) / 2.0,
        position * (position - 1.0) * (position - 2.0) / 6.0,
    ]


def gather_point(quads, column, row):
    cell = (row & (BH - 1)) * BW + (column & (BW - 1))
    right = column >= BW
    lower = row >= BH
    picked = []
    for parts in zip(*quads):
        g = [jnp.take_along_axis(x, cell, axis=1, mode="promise_in_bounds") for x in parts]
        picked.append(jnp.where(lower, jnp.where(right, g[3], g[2]), jnp.where(right, g[1], g[0])))
    return picked


def kernel(
    n_tile, n_lev, nblocks,
    regions, far_start, base_ref, wind_ref, tracer_ref,
    new_ref, disp_ref,
    wbuf, tbuf, ebuf, pack, edge, edge_pack,
    send_sem, recv_sem,
):
    half = nblocks // 2
    quarter = half // 2
    band = lax.axis_index("tile")
    lev = lax.axis_index("lev")

    def exists(d, e):
        ok = None
        if d < 0:
            ok = band >= -d
        elif d > 0:
            ok = band < n_tile - d
        if e:
            side = lev >= 1 if e < 0 else lev < n_lev - 1
            ok = side if ok is None else jnp.logical_and(ok, side)
        return ok

    partners = [(d, e) for e in (0, -1, 1) for d in (0, -1, 1, -2, 2) if (d, e) != (0, 0)]
    barrier = pltpu.get_barrier_semaphore()
    for d, e in partners:
        @pl.when(exists(d, e))
        def _(d=d, e=e):
            pl.semaphore_signal(barrier, inc=1, device_id=(band + d, lev + e), device_id_type=MESH)

    slot_of = {-2: 0, -1: half, 0: half + nblocks, 1: half + 2 * nblocks, 2: half + 3 * nblocks}

    starts = [far_start[ITERS, band, 0], far_start[ITERS, band, 1]]
    wbuf[2] = wind_ref[...]

    def pack_step(j, carry):
        for side in (0, 1):
            for i in (0, 1):
                block = tracer_ref[lax.rem(starts[side] + 2 * j + i, nblocks)]
                pack[side, 2 * j + i] = block
                wide = block.astype(jnp.float32)
                if i == 0:
                    first = wide
            low = jnp.concatenate([first[0:8], wide[0:8]], axis=0)
            top = jnp.concatenate([first[24:32], wide[24:32]], axis=0)
            edge_pack[0, side, j] = low.astype(jnp.bfloat16)
            edge_pack[1, side, j] = top.astype(jnp.bfloat16)
        return carry

    def edge_step(j, carry):
        first = tracer_ref[2 * j].astype(jnp.float32)
        second = tracer_ref[2 * j + 1].astype(jnp.float32)
        edge[0, j] = jnp.concatenate([first[0:8], second[0:8]], axis=0).astype(jnp.bfloat16)
        edge[1, j] = jnp.concatenate([first[24:32], second[24:32]], axis=0).astype(jnp.bfloat16)
        return carry

    own = slot_of[0]
    tbuf[own : own + nblocks] = tracer_ref[...]
    lax.fori_loop(0, quarter, pack_step, 0)
    lax.fori_loop(0, half, edge_step, 0)

    count = jnp.int32(0)
    for d, e in partners:
        count = count + exists(d, e).astype(jnp.int32)
    pl.semaphore_wait(barrier, count)

    wind_copies, tracer_copies = [], []

    def add(listed, d, e, src, dst):
        at = len(wind_copies) + len(tracer_copies)
        copy = pltpu.make_async_remote_copy(
            src_ref=src, dst_ref=dst, send_sem=send_sem.at[at], recv_sem=recv_sem.at[at],
            device_id=(band + d, lev + e), device_id_type=MESH,
        )
        listed.append((copy, exists(d, e), exists(-d, -e)))

    for d in (-1, 1, -2, 2):
        add(wind_copies, d, 0, wind_ref, wbuf.at[2 - d])
    for d in (-1, 1):
        add(tracer_copies, d, 0, tracer_ref, tbuf.at[pl.ds(slot_of[-d], nblocks)])
    for d in (-2, 2):
        add(tracer_copies, d, 0, pack.at[0 if d > 0 else 1], tbuf.at[pl.ds(slot_of[-d], half)])
    for e in (-1, 1):
        mine = 0 if e < 0 else 1
        theirs = 1 - mine
        for d in (0, -1, 1):
            add(tracer_copies, d, e, edge.at[mine], ebuf.at[theirs, pl.ds(slot_of[-d] // 2, half)])
        for d in (-2, 2):
            add(
                tracer_copies, d, e, edge_pack.at[mine, 0 if d > 0 else 1],
                ebuf.at[theirs, pl.ds(slot_of[-d] // 2, quarter)],
            )
    for copy, sends, _ in wind_copies + tracer_copies:
        @pl.when(sends)
        def _(copy=copy):
            copy.start()

    def drain_recv(copies):
        for copy, _, receives in copies:
            @pl.when(receives)
            def _(copy=copy):
                copy.wait_recv()

    def reads(section, block):
        low = far_start[section, jnp.maximum(band - 2, 0), 0]
        high = far_start[section, jnp.minimum(band + 2, n_tile - 1), 1]
        upper = regions[section, block, 0]
        left = regions[section, block, 1]
        listed = []
        for quad_y in (0, 1):
            for quad_x in (0, 1):
                offset = jnp.clip(upper + quad_y - band, -2, 2)
                col = lax.rem(left + quad_x, nblocks)
                run_low = lax.rem(col - low + nblocks, nblocks)
                run_high = lax.rem(col - high + nblocks, nblocks)
                outside = jnp.logical_or(
                    jnp.logical_and(offset == -2, run_low >= half),
                    jnp.logical_and(offset == 2, run_high >= half),
                )
                inside = jnp.where(outside, 0.0, 1.0).astype(jnp.float32)
                slot = jnp.where(
                    offset == -2,
                    jnp.minimum(run_low, half - 1),
                    jnp.where(
                        offset == 2,
                        half + 3 * nblocks + jnp.minimum(run_high, half - 1),
                        half + (offset + 1) * nblocks + col,
                    ),
                )
                listed.append((offset + 2, col, slot, inside))
        return listed

    def wind_step(block, carry):
        arrive = wind_ref[block].astype(jnp.float32)
        own_parts = [arrive[0:8], arrive[8:16]]
        top_rows = lax.broadcasted_iota(jnp.int32, (8, BW * BH), 0) < 4
        displace = [jnp.zeros((8, BW * BH), jnp.float32)] * 2
        for section in range(ITERS):
            quads = []
            for band_at, col, _, inside in reads(section, block):
                x = wbuf[band_at, col].astype(jnp.float32) * inside
                quads.append([x[0:8], x[8:16]])
            bx = jnp.broadcast_to(base_ref[section, 0, pl.ds(block, 1), :], (8, BW * BH))
            by = jnp.broadcast_to(base_ref[section, 1, pl.ds(block, 1), :], (8, BW * BH))
            frac = 0.5 + 0.5 * jnp.tanh(displace[0])
            turned = jnp.concatenate([frac[4:8], frac[0:4]], axis=0)
            fx = jnp.where(top_rows, frac, turned)
            fy = jnp.where(top_rows, turned, frac)
            total = None
            for b, wy in ((0, 1.0 - fy), (1, fy)):
                for a, wx in ((0, 1.0 - fx), (1, fx)):
                    w = wx * wy
                    got = [w * g for g in gather_point(quads, bx + (1 + a), by + (1 + b))]
                    total = got if total is None else [t + g for t, g in zip(total, got)]
            displace = [0.5 * (o + t) for o, t in zip(own_parts, total)]
        disp_ref[block] = jnp.concatenate(displace, axis=0)
        return carry

    drain_recv(wind_copies)
    lax.fori_loop(0, nblocks, wind_step, 0)
    drain_recv(tracer_copies)

    def tracer_step(block, carry):
        quads = []
        for _, _, slot, inside in reads(ITERS, block):
            x = tbuf[slot].astype(jnp.float32) * inside
            levels = [x[8 * l : 8 * l + 8] for l in range(4)]
            odd = lax.rem(slot, 2) == 1
            pair = lax.div(slot, 2)
            below = ebuf[0, pair].astype(jnp.float32)
            above = ebuf[1, pair].astype(jnp.float32)
            below = jnp.where(lev == 0, levels[0], jnp.where(odd, below[8:16], below[0:8]) * inside)
            above = jnp.where(lev == n_lev - 1, levels[3], jnp.where(odd, above[8:16], above[0:8]) * inside)
            quads.append([below] + levels + [above])
        shape = (8, BW * BH)
        bx = jnp.broadcast_to(base_ref[ITERS, 0, pl.ds(block, 1), :], shape)
        by = jnp.broadcast_to(base_ref[ITERS, 1, pl.ds(block, 1), :], shape)
        bent = jnp.tanh(disp_ref[block])
        lx = lagrange_cubic(1.5 + 0.5 * bent[0:8])
        ly = lagrange_cubic(1.5 + 0.5 * bent[0:8])
        s = bent[8:16]
        up = [0.5 * s * (s - 1.0), 1.0 - s * s, 0.5 * s * (s + 1.0)]

        def row(x, at):
            return jnp.broadcast_to(x[at : at + 1], shape)

        wx = [[row(x, l) for x in lx] for l in range(4)]
        wy = [[row(y, 4 + l) for y in ly] for l in range(4)]
        wv = [[row(v, l) for v in up] for l in range(4)]
        total = [None] * 4
        for n in range(4):
            for m in range(4):
                g = gather_point(quads, bx + m, by + n)
                for l in range(4):
                    h = wv[l][0] * g[l] + wv[l][1] * g[l + 1] + wv[l][2] * g[l + 2]
                    h = h * (wx[l][m] * wy[l][n])
                    total[l] = h if total[l] is None else total[l] + h
        new_ref[block] = jnp.concatenate(total, axis=0).astype(jnp.bfloat16)
        return carry

    lax.fori_loop(0, nblocks, tracer_step, 0)
    for copy, sends, _ in wind_copies + tracer_copies:
        @pl.when(sends)
        def _(copy=copy):
            copy.wait_send()


def body(tracers, wind_field, regions, stencil_base, far_start):
    n_tracer, n_level, nblocks, cells = tracers.shape
    n_tile, n_lev = lax.axis_size("tile"), lax.axis_size("lev")
    wind = jnp.transpose(wind_field.reshape(3 * n_level, nblocks, cells), (1, 0, 2))
    wind = jnp.pad(wind, ((0, 0), (0, 16 - 3 * n_level), (0, 0)))
    tracer = jnp.transpose(tracers, (2, 1, 0, 3)).reshape(nblocks, n_level * n_tracer, cells)
    rows = n_level * n_tracer
    half = nblocks // 2
    vmem = pl.BlockSpec(memory_space=pltpu.VMEM)
    smem = pl.BlockSpec(memory_space=pltpu.SMEM)
    new, disp = pl.pallas_call(
        functools.partial(kernel, n_tile, n_lev, nblocks),
        out_shape=(
            jax.ShapeDtypeStruct((nblocks, rows, cells), jnp.bfloat16),
            jax.ShapeDtypeStruct((nblocks, 16, cells), jnp.float32),
        ),
        in_specs=[smem, smem, vmem, vmem, vmem],
        out_specs=(vmem, vmem),
        scratch_shapes=[
            pltpu.VMEM((5, nblocks, 16, cells), jnp.bfloat16),
            pltpu.VMEM((4 * nblocks, rows, cells), jnp.bfloat16),
            pltpu.VMEM((2, 2 * nblocks, 16, cells), jnp.bfloat16),
            pltpu.VMEM((2, half, rows, cells), jnp.bfloat16),
            pltpu.VMEM((2, half, 16, cells), jnp.bfloat16),
            pltpu.VMEM((2, 2, half // 2, 16, cells), jnp.bfloat16),
            pltpu.SemaphoreType.DMA((18,)),
            pltpu.SemaphoreType.DMA((18,)),
        ],
        compiler_params=pltpu.CompilerParams(
            collective_id=0, has_side_effects=True, vmem_limit_bytes=32 * 1024 * 1024
        ),
    )(regions, far_start, stencil_base, wind, tracer)
    tracers_new = jnp.transpose(new.reshape(nblocks, n_level, n_tracer, cells), (2, 1, 0, 3))
    displacement = jnp.transpose(disp[:, : 3 * n_level], (1, 0, 2)).reshape(3, n_level, nblocks, cells)
    return tracers_new, displacement


def solution(mesh):
    return jax.shard_map(
        body,
        mesh=mesh,
        in_specs=(
            P(None, "lev", "tile", None),
            P(None, "lev", "tile", None),
            P(None, "tile", None),
            P(None, None, "tile", None),
            P(),
        ),
        out_specs=(P(None, "lev", "tile", None), P(None, "lev", "tile", None)),
        check_vma=False,
    )
```

profile of v0, /device:TPU:8, one launch (start us, length us, event | category | flops | bytes accessed | tf_op | source)
XLA Modules:
  0.0 33.1 jit_solution(16700030333727302726)
XLA Ops:
  0.6 0.0 copy-start.2
  0.6 0.8 %copy.15.regions = s32[4,16,2]{2,1,0:T(8,128)S(1)} copy(s32[4,16,2]{1,2,0:T(2,128)} %param.7) | data formatting | bytes 1024 | tf_op args[2]
  1.4 0.8 %copy.16.far_start = s32[4,16,2]{2,1,0:T(8,128)S(1)} copy(s32[4,16,2]{1,2,0:T(2,128)} %param.9) | data formatting | bytes 1024 | tf_op args[4]
  2.2 0.0 copy-done.2
  2.2 0.0 copy-start.1
  2.3 0.9 %copy-done.1 = bf16[8,4,16,128]{3,2,1,0:T(8,128)(2,1)S(1)} copy-done((bf16[8,4,16,128]{3,2,1,0:T(8,128)(2,1)S(1)}, bf16[8,4,16,128]{3,2,1,0:T(8,128)(2,1)}, u32[]{:S(2)}) %copy-start.1) | copy-done | bytes 131096
  3.1 0.0 copy-start
  3.1 0.1 copy.23
  3.2 0.7 %copy-done = s32[4,2,16,128]{3,2,1,0:T(8,128)S(1)} copy-done((s32[4,2,16,128]{3,2,1,0:T(8,128)S(1)}, s32[4,2,16,128]{3,2,1,0:T(8,128)}, u32[]{:S(2)}) %copy-start) | copy-done | bytes 65560
  4.0 27.7 %shard_map.68 = (bf16[16,32,128]{2,1,0:T(8,128)(2,1)S(1)}, f32[16,16,128]{2,1,0:T(8,128)S(1)}) custom-call(s32[4,16,2]{2,1,0:T(8,128)S(1)} %copy.15.regions, s32[4,16,2]{2,1,0:T(8,128)S(1)} %copy.16.far_start, s32[4,2,16,128]{3,2,1,0:T(8,128)S(1)} %copy-done, bf16[16,16,128]{2,1,0:T(8,128)(2,1)S(1)} %pad.4.wind_ref, bf16[16,32,128]{2,1,0:T(8,128)(2,1)S(1)} %bitcast.15), custom_call_target="tpu_custom_call" | custom-call | tf_op jit(solution)/shard_map/pallas_call | solution.py:253
  31.7 0.7 %copy.22 = bf16[16,4,8,128]{3,0,1,2:T(8,128)(2,1)} copy(bf16[16,4,8,128]{3,2,1,0:T(8,128)(2,1)S(1)} %bitcast.16) | data formatting | bytes 262144 | tf_op jit(solution)/shard_map/reshape | solution.py:275
  32.4 0.7 %copy.18 = f32[12,16,128]{2,1,0:T(8,128)} copy(f32[12,16,128]{2,0,1:T(8,128)S(1)} %slice_bitcast_fusion) | data formatting | bytes 196608 | tf_op jit(solution)/shard_map/transpose | solution.py:276
  (3 shorter events, 0.0 us)
Async XLA Ops:
  0.6 1.6 %copy-start.2 = (bf16[3,4,16,128]{3,2,1,0:T(8,128)(2,1)S(1)}, bf16[3,4,16,128]{3,2,1,0:T(8,128)(2,1)}, u32[]{:S(2)}) copy-start(bf16[3,4,16,128]{3,2,1,0:T(8,128)(2,1)} %param.6) | copy-start | bytes 147460
  2.2 0.9 %copy-start.1 = (bf16[8,4,16,128]{3,2,1,0:T(8,128)(2,1)S(1)}, bf16[8,4,16,128]{3,2,1,0:T(8,128)(2,1)}, u32[]{:S(2)}) copy-start(bf16[8,4,16,128]{3,2,1,0:T(8,128)(2,1)} %param.5) | copy-start | bytes 393220
  3.1 0.8 %copy-start = (s32[4,2,16,128]{3,2,1,0:T(8,128)S(1)}, s32[4,2,16,128]{3,2,1,0:T(8,128)}, u32[]{:S(2)}) copy-start(s32[4,2,16,128]{3,2,1,0:T(8,128)} %base_ref.1) | copy-start | bytes 196612
where the time goes:
time: 33.4 us; the launch traced here: 33.1 us
  Pallas kernels  27.7 us (83%)
  local copies, waits for them, and re-layouts  4.69 us (14%)
  between operations  0.67 us (2%)
    pallas_call x1, Pallas kernels, body(): pl.pallas_call(functools.partial(kernel, n_tile, n_lev, nblocks), out_sha...  27.7 us
    unnamed x8, local copies, waits for them, and re-layouts  3.18 us
    reshape x1, local copies, waits for them, and re-layouts, body(): new.reshape(nblocks, n_level, n_tracer, cells)  0.71 us
    transpose x2, local copies, waits for them, and re-layouts, body(): jnp.transpose(disp[:, :3 * n_level], (1, 0, 2))  0.68 us

commit v1 on v0

--- a/solution.py
+++ b/solution.py
@@ -35,10 +35,10 @@
 
 def kernel(
     n_tile, n_lev, nblocks,
-    regions, far_start, base_ref, wind_ref, tracer_ref,
+    regions, far_start, base_hbm, wind_ref, tracer_ref,
     new_ref, disp_ref,
-    wbuf, tbuf, ebuf, pack, edge, edge_pack,
-    send_sem, recv_sem,
+    wbuf, tbuf, ebuf, pack, edge, edge_pack, base_ref,
+    send_sem, recv_sem, base_sem,
 ):
     half = nblocks // 2
     quarter = half // 2
@@ -65,7 +65,7 @@
 
     slot_of = {-2: 0, -1: half, 0: half + nblocks, 1: half + 2 * nblocks, 2: half + 3 * nblocks}
 
-    starts = [far_start[ITERS, band, 0], far_start[ITERS, band, 1]]
+    starts = [far_start[ITERS, 0, band], far_start[ITERS, 1, band]]
     wbuf[2] = wind_ref[...]
 
     def pack_step(j, carry):
@@ -91,8 +91,8 @@
 
     own = slot_of[0]
     tbuf[own : own + nblocks] = tracer_ref[...]
-    lax.fori_loop(0, quarter, pack_step, 0)
-    lax.fori_loop(0, half, edge_step, 0)
+    base_copy = pltpu.make_async_copy(base_hbm, base_ref, base_sem)
+    base_copy.start()
 
     count = jnp.int32(0)
     for d, e in partners:
@@ -125,10 +125,19 @@
                 tracer_copies, d, e, edge_pack.at[mine, 0 if d > 0 else 1],
                 ebuf.at[theirs, pl.ds(slot_of[-d] // 2, quarter)],
             )
-    for copy, sends, _ in wind_copies + tracer_copies:
-        @pl.when(sends)
-        def _(copy=copy):
-            copy.start()
+    def start(copies):
+        for copy, sends, _ in copies:
+            @pl.when(sends)
+            def _(copy=copy):
+                copy.start()
+
+    start(wind_copies)
+    start(tracer_copies[:2])
+    lax.fori_loop(0, quarter, pack_step, 0, unroll=2)
+    start(tracer_copies[2:4])
+    lax.fori_loop(0, half, edge_step, 0, unroll=2)
+    start(tracer_copies[4:])
+    base_copy.wait()
 
     def drain_recv(copies):
         for copy, _, receives in copies:
@@ -137,10 +146,10 @@
                 copy.wait_recv()
 
     def reads(section, block):
-        low = far_start[section, jnp.maximum(band - 2, 0), 0]
-        high = far_start[section, jnp.minimum(band + 2, n_tile - 1), 1]
-        upper = regions[section, block, 0]
-        left = regions[section, block, 1]
+        low = far_start[section, 0, jnp.maximum(band - 2, 0)]
+        high = far_start[section, 1, jnp.minimum(band + 2, n_tile - 1)]
+        upper = regions[section, 0, block]
+        left = regions[section, 1, block]
         listed = []
         for quad_y in (0, 1):
             for quad_x in (0, 1):
@@ -192,7 +201,7 @@
         return carry
 
     drain_recv(wind_copies)
-    lax.fori_loop(0, nblocks, wind_step, 0)
+    lax.fori_loop(0, nblocks, wind_step, 0, unroll=4)
     drain_recv(tracer_copies)
 
     def tracer_step(block, carry):
@@ -233,7 +242,7 @@
         new_ref[block] = jnp.concatenate(total, axis=0).astype(jnp.bfloat16)
         return carry
 
-    lax.fori_loop(0, nblocks, tracer_step, 0)
+    lax.fori_loop(0, nblocks, tracer_step, 0, unroll=2)
     for copy, sends, _ in wind_copies + tracer_copies:
         @pl.when(sends)
         def _(copy=copy):
@@ -256,7 +265,7 @@
             jax.ShapeDtypeStruct((nblocks, rows, cells), jnp.bfloat16),
             jax.ShapeDtypeStruct((nblocks, 16, cells), jnp.float32),
         ),
-        in_specs=[smem, smem, vmem, vmem, vmem],
+        in_specs=[smem, smem, pl.BlockSpec(memory_space=pl.ANY), vmem, vmem],
         out_specs=(vmem, vmem),
         scratch_shapes=[
             pltpu.VMEM((5, nblocks, 16, cells), jnp.bfloat16),
@@ -265,13 +274,15 @@
             pltpu.VMEM((2, half, rows, cells), jnp.bfloat16),
             pltpu.VMEM((2, half, 16, cells), jnp.bfloat16),
             pltpu.VMEM((2, 2, half // 2, 16, cells), jnp.bfloat16),
+            pltpu.VMEM(stencil_base.shape, jnp.int32),
             pltpu.SemaphoreType.DMA((18,)),
             pltpu.SemaphoreType.DMA((18,)),
+            pltpu.SemaphoreType.DMA,
         ],
         compiler_params=pltpu.CompilerParams(
             collective_id=0, has_side_effects=True, vmem_limit_bytes=32 * 1024 * 1024
         ),
-    )(regions, far_start, stencil_base, wind, tracer)
+    )(jnp.transpose(regions, (0, 2, 1)), jnp.transpose(far_start, (0, 2, 1)), stencil_base, wind, tracer)
     tracers_new = jnp.transpose(new.reshape(nblocks, n_level, n_tracer, cells), (2, 1, 0, 3))
     displacement = jnp.transpose(disp[:, : 3 * n_level], (1, 0, 2)).reshape(3, n_level, nblocks, cells)
     return tracers_new, displacement

time: 33.4 us -> 29.3 us (0.88)
  the two profiles are of different devices: /device:TPU:8 before, /device:TPU:9 now
where the time goes in v1:
time: 29.3 us; the launch traced here: 29 us
  Pallas kernels  25.2 us (86%)
  local copies, waits for them, and re-layouts  3.14 us (11%)
  between operations  0.67 us (2%)
    pallas_call x1, Pallas kernels, body(): pl.pallas_call(functools.partial(kernel, n_tile, n_lev, nblocks), out_sha...  25.2 us
    reshape x1, local copies, waits for them, and re-layouts, body(): wind_field.reshape(3 * n_level, nblocks, cells)  0.85 us
    unnamed x8, local copies, waits for them, and re-layouts  0.79 us
    reshape x1, local copies, waits for them, and re-layouts, body(): new.reshape(nblocks, n_level, n_tracer, cells)  0.71 us
    transpose x2, local copies, waits for them, and re-layouts, body(): jnp.transpose(disp[:, :3 * n_level], (1, 0, 2))  0.68 us

profile of v1, /device:TPU:9, one launch (start us, length us, event | category | flops | bytes accessed | tf_op | source)
XLA Modules:
  0.0 29.0 jit_solution(7281854539696375897)
XLA Ops:
  0.6 0.0 copy-start.3
  0.6 0.8 %copy.20 = bf16[12,16,128]{2,0,1:T(8,128)(2,1)S(1)} copy(bf16[12,16,128]{2,1,0:T(8,128)(2,1)} %bitcast.25) | data formatting | bytes 98304 | tf_op jit(solution)/shard_map/reshape | solution.py:255
  1.5 0.0 copy-done.3
  1.6 0.0 copy-start
  1.6 0.0 copy-start.1
  1.6 0.0 copy-start.2
  1.6 0.1 copy.19
  1.7 0.7 %copy-done = s32[4,2,16,128]{3,2,1,0:T(8,128)S(1)} copy-done((s32[4,2,16,128]{3,2,1,0:T(8,128)S(1)}, s32[4,2,16,128]{3,2,1,0:T(8,128)}, u32[]{:S(2)}) %copy-start) | copy-done | bytes 65560
  2.4 0.0 copy-done.1
  2.4 0.0 copy-done.2
  2.4 25.2 %shard_map.68 = (bf16[16,32,128]{2,1,0:T(8,128)(2,1)S(1)}, f32[16,16,128]{2,1,0:T(8,128)S(1)}) custom-call(s32[4,2,16]{2,1,0:T(2,128)S(1)} %bitcast.19, s32[4,2,16]{2,1,0:T(2,128)S(1)} %bitcast.20, s32[4,2,16,128]{3,2,1,0:T(8,128)S(1)} %copy-done, bf16[16,16,128]{2,1,0:T(8,128)(2,1)S(1)} %pad.4.wind_ref, bf16[16,32,128]{2,1,0:T(8,128)(2,1)S(1)} %bitcast.17), custom_call_target="tpu_custom_call" | custom-call | tf_op jit(solution)/shard_map/pallas_call | solution.py:262
  27.6 0.7 %copy.18 = bf16[16,4,8,128]{3,0,1,2:T(8,128)(2,1)} copy(bf16[16,4,8,128]{3,2,1,0:T(8,128)(2,1)S(1)} %bitcast.18) | data formatting | bytes 262144 | tf_op jit(solution)/shard_map/reshape | solution.py:286
  28.3 0.7 %copy.14 = f32[12,16,128]{2,1,0:T(8,128)} copy(f32[12,16,128]{2,0,1:T(8,128)S(1)} %slice_bitcast_fusion) | data formatting | bytes 196608 | tf_op jit(solution)/shard_map/transpose | solution.py:287
  (2 shorter events, 0.0 us)
Async XLA Ops:
  0.6 0.9 %copy-start.3 = (bf16[8,4,16,128]{3,2,1,0:T(8,128)(2,1)S(1)}, bf16[8,4,16,128]{3,2,1,0:T(8,128)(2,1)}, u32[]{:S(2)}) copy-start(bf16[8,4,16,128]{3,2,1,0:T(8,128)(2,1)} %param.5) | copy-start | bytes 393220
  1.6 0.8 %copy-start = (s32[4,2,16,128]{3,2,1,0:T(8,128)S(1)}, s32[4,2,16,128]{3,2,1,0:T(8,128)}, u32[]{:S(2)}) copy-start(s32[4,2,16,128]{3,2,1,0:T(8,128)} %base_hbm.1) | copy-start | bytes 196612
  1.6 0.8 %copy-start.1 = (s32[4,16,2]{1,2,0:T(2,128)S(1)}, s32[4,16,2]{1,2,0:T(2,128)}, u32[]{:S(2)}) copy-start(s32[4,16,2]{1,2,0:T(2,128)} %param.7) | copy-start | bytes 1540
  1.6 0.8 %copy-start.2 = (s32[4,16,2]{1,2,0:T(2,128)S(1)}, s32[4,16,2]{1,2,0:T(2,128)}, u32[]{:S(2)}) copy-start(s32[4,16,2]{1,2,0:T(2,128)} %param.9) | copy-start | bytes 1540

commit v2 on v1

--- a/solution.py
+++ b/solution.py
@@ -63,7 +63,9 @@
         def _(d=d, e=e):
             pl.semaphore_signal(barrier, inc=1, device_id=(band + d, lev + e), device_id_type=MESH)
 
-    slot_of = {-2: 0, -1: half, 0: half + nblocks, 1: half + 2 * nblocks, 2: half + 3 * nblocks}
+    slot_of = {d: (d + 2) * nblocks for d in range(-2, 3)}
+    even = lax.rem(band, 2) == 0
+    odd = lax.rem(band, 2) == 1
 
     starts = [far_start[ITERS, 0, band], far_start[ITERS, 1, band]]
     wbuf[2] = wind_ref[...]
@@ -101,13 +103,31 @@
 
     wind_copies, tracer_copies = [], []
 
-    def add(listed, d, e, src, dst):
-        at = len(wind_copies) + len(tracer_copies)
+    def add(listed, d, e, src, dst, sends=None, receives=None):
+        at = len(wind_copies) + len(tracer_copies) + len(wind_relays) + len(tracer_relays)
         copy = pltpu.make_async_remote_copy(
             src_ref=src, dst_ref=dst, send_sem=send_sem.at[at], recv_sem=recv_sem.at[at],
             device_id=(band + d, lev + e), device_id_type=MESH,
         )
-        listed.append((copy, exists(d, e), exists(-d, -e)))
+        if sends is None:
+            sends, receives = exists(d, e), exists(-d, -e)
+            if abs(d) == 2:
+                side = even if d > 0 else odd
+                sends, receives = jnp.logical_and(sends, side), jnp.logical_and(receives, side)
+        listed.append((copy, sends, receives))
+
+    wind_relays, tracer_relays = [], []
+
+    def relay(listed, buffer, at_of, size, allowed=None):
+        for d, mine, to in ((1, even, odd), (-1, odd, even)):
+            sends = jnp.logical_and(mine, band >= 1 if d > 0 else band < n_tile - 1)
+            receives = jnp.logical_and(to, band >= 2 if d > 0 else band < n_tile - 2)
+            if allowed is not None:
+                sends, receives = jnp.logical_and(sends, allowed), jnp.logical_and(receives, allowed)
+            add(
+                listed, d, 0, buffer.at[pl.ds(at_of(-d), size)],
+                buffer.at[pl.ds(at_of(-2 * d), size)], sends, receives,
+            )
 
     for d in (-1, 1, -2, 2):
         add(wind_copies, d, 0, wind_ref, wbuf.at[2 - d])
@@ -125,6 +145,11 @@
                 tracer_copies, d, e, edge_pack.at[mine, 0 if d > 0 else 1],
                 ebuf.at[theirs, pl.ds(slot_of[-d] // 2, quarter)],
             )
+    relay(wind_relays, wbuf, lambda d: d + 2, 1)
+    relay(tracer_relays, tbuf, lambda d: slot_of[d], nblocks)
+    relay(tracer_relays, ebuf.at[0], lambda d: slot_of[d] // 2, half, lev >= 1)
+    relay(tracer_relays, ebuf.at[1], lambda d: slot_of[d] // 2, half, lev < n_lev - 1)
+
     def start(copies):
         for copy, sends, _ in copies:
             @pl.when(sends)
@@ -162,15 +187,14 @@
                     jnp.logical_and(offset == 2, run_high >= half),
                 )
                 inside = jnp.where(outside, 0.0, 1.0).astype(jnp.float32)
-                slot = jnp.where(
-                    offset == -2,
+                place = jnp.where(
+                    jnp.logical_and(offset == -2, even),
                     jnp.minimum(run_low, half - 1),
                     jnp.where(
-                        offset == 2,
-                        half + 3 * nblocks + jnp.minimum(run_high, half - 1),
-                        half + (offset + 1) * nblocks + col,
+                        jnp.logical_and(offset == 2, odd), jnp.minimum(run_high, half - 1), col
                     ),
                 )
+                slot = (offset + 2) * nblocks + place
                 listed.append((offset + 2, col, slot, inside))
         return listed
 
@@ -201,8 +225,14 @@
         return carry
 
     drain_recv(wind_copies)
-    lax.fori_loop(0, nblocks, wind_step, 0, unroll=4)
+    start(wind_relays)
+    drain_recv(wind_relays)
+    ahead = 3 * nblocks // 4
+    lax.fori_loop(0, ahead, wind_step, 0, unroll=4)
     drain_recv(tracer_copies)
+    start(tracer_relays)
+    lax.fori_loop(ahead, nblocks, wind_step, 0, unroll=4)
+    drain_recv(tracer_relays)
 
     def tracer_step(block, carry):
         quads = []
@@ -243,7 +273,7 @@
         return carry
 
     lax.fori_loop(0, nblocks, tracer_step, 0, unroll=2)
-    for copy, sends, _ in wind_copies + tracer_copies:
+    for copy, sends, _ in wind_copies + tracer_copies + wind_relays + tracer_relays:
         @pl.when(sends)
         def _(copy=copy):
             copy.wait_send()
@@ -269,14 +299,14 @@
         out_specs=(vmem, vmem),
         scratch_shapes=[
             pltpu.VMEM((5, nblocks, 16, cells), jnp.bfloat16),
-            pltpu.VMEM((4 * nblocks, rows, cells), jnp.bfloat16),
-            pltpu.VMEM((2, 2 * nblocks, 16, cells), jnp.bfloat16),
+            pltpu.VMEM((5 * nblocks, rows, cells), jnp.bfloat16),
+            pltpu.VMEM((2, 5 * half, 16, cells), jnp.bfloat16),
             pltpu.VMEM((2, half, rows, cells), jnp.bfloat16),
             pltpu.VMEM((2, half, 16, cells), jnp.bfloat16),
             pltpu.VMEM((2, 2, half // 2, 16, cells), jnp.bfloat16),
             pltpu.VMEM(stencil_base.shape, jnp.int32),
-            pltpu.SemaphoreType.DMA((18,)),
-            pltpu.SemaphoreType.DMA((18,)),
+            pltpu.SemaphoreType.DMA((26,)),
+            pltpu.SemaphoreType.DMA((26,)),
             pltpu.SemaphoreType.DMA,
         ],
         compiler_params=pltpu.CompilerParams(

time: 29.3 us -> 27.6 us (0.942)
  Pallas kernels: 25.2 us -> 23.6 us
    pallas_call x1, Pallas kernels: 25.2 us -> 23.6 us  [body(): pl.pallas_call(functools.partial(kernel, n_tile, n_lev, nblocks), out_sha...]
where the time goes in v2:
time: 27.6 us; the launch traced here: 27.4 us
  Pallas kernels  23.6 us (86%)
  local copies, waits for them, and re-layouts  3.14 us (11%)
  between operations  0.67 us (2%)
    pallas_call x1, Pallas kernels, body(): pl.pallas_call(functools.partial(kernel, n_tile, n_lev, nblocks), out_sha...  23.6 us
    reshape x1, local copies, waits for them, and re-layouts, body(): wind_field.reshape(3 * n_level, nblocks, cells)  0.85 us
    unnamed x8, local copies, waits for them, and re-layouts  0.79 us
    reshape x1, local copies, waits for them, and re-layouts, body(): new.reshape(nblocks, n_level, n_tracer, cells)  0.71 us
    transpose x2, local copies, waits for them, and re-layouts, body(): jnp.transpose(disp[:, :3 * n_level], (1, 0, 2))  0.68 us

profile of v2, /device:TPU:9, one launch (start us, length us, event | category | flops | bytes accessed | tf_op | source)
XLA Modules:
  0.0 27.4 jit_solution(15012062345852525137)
XLA Ops:
  0.6 0.0 copy-start.3
  0.6 0.8 %copy.20 = bf16[12,16,128]{2,0,1:T(8,128)(2,1)S(1)} copy(bf16[12,16,128]{2,1,0:T(8,128)(2,1)} %bitcast.25) | data formatting | bytes 98304 | tf_op jit(solution)/shard_map/reshape | solution.py:285
  1.5 0.0 copy-done.3
  1.6 0.0 copy-start
  1.6 0.0 copy-start.1
  1.6 0.0 copy-start.2
  1.6 0.1 copy.19
  1.7 0.7 %copy-done = s32[4,2,16,128]{3,2,1,0:T(8,128)S(1)} copy-done((s32[4,2,16,128]{3,2,1,0:T(8,128)S(1)}, s32[4,2,16,128]{3,2,1,0:T(8,128)}, u32[]{:S(2)}) %copy-start) | copy-done | bytes 65560
  2.4 0.0 copy-done.1
  2.4 0.0 copy-done.2
  2.4 23.6 %shard_map.68 = (bf16[16,32,128]{2,1,0:T(8,128)(2,1)S(1)}, f32[16,16,128]{2,1,0:T(8,128)S(1)}) custom-call(s32[4,2,16]{2,1,0:T(2,128)S(1)} %bitcast.19, s32[4,2,16]{2,1,0:T(2,128)S(1)} %bitcast.20, s32[4,2,16,128]{3,2,1,0:T(8,128)S(1)} %copy-done, bf16[16,16,128]{2,1,0:T(8,128)(2,1)S(1)} %pad.4.wind_ref, bf16[16,32,128]{2,1,0:T(8,128)(2,1)S(1)} %bitcast.17), custom_call_target="tpu_custom_call" | custom-call | tf_op jit(solution)/shard_map/pallas_call | solution.py:292
  26.0 0.7 %copy.18 = bf16[16,4,8,128]{3,0,1,2:T(8,128)(2,1)} copy(bf16[16,4,8,128]{3,2,1,0:T(8,128)(2,1)S(1)} %bitcast.18) | data formatting | bytes 262144 | tf_op jit(solution)/shard_map/reshape | solution.py:316
  26.7 0.7 %copy.14 = f32[12,16,128]{2,1,0:T(8,128)} copy(f32[12,16,128]{2,0,1:T(8,128)S(1)} %slice_bitcast_fusion) | data formatting | bytes 196608 | tf_op jit(solution)/shard_map/transpose | solution.py:317
  (2 shorter events, 0.0 us)
Async XLA Ops:
  0.6 0.9 %copy-start.3 = (bf16[8,4,16,128]{3,2,1,0:T(8,128)(2,1)S(1)}, bf16[8,4,16,128]{3,2,1,0:T(8,128)(2,1)}, u32[]{:S(2)}) copy-start(bf16[8,4,16,128]{3,2,1,0:T(8,128)(2,1)} %param.5) | copy-start | bytes 393220
  1.6 0.8 %copy-start = (s32[4,2,16,128]{3,2,1,0:T(8,128)S(1)}, s32[4,2,16,128]{3,2,1,0:T(8,128)}, u32[]{:S(2)}) copy-start(s32[4,2,16,128]{3,2,1,0:T(8,128)} %base_hbm.1) | copy-start | bytes 196612
  1.6 0.8 %copy-start.1 = (s32[4,16,2]{1,2,0:T(2,128)S(1)}, s32[4,16,2]{1,2,0:T(2,128)}, u32[]{:S(2)}) copy-start(s32[4,16,2]{1,2,0:T(2,128)} %param.7) | copy-start | bytes 1540
  1.6 0.8 %copy-start.2 = (s32[4,16,2]{1,2,0:T(2,128)S(1)}, s32[4,16,2]{1,2,0:T(2,128)}, u32[]{:S(2)}) copy-start(s32[4,16,2]{1,2,0:T(2,128)} %param.9) | copy-start | bytes 1540

commit v3 on v2

--- a/solution.py
+++ b/solution.py
@@ -263,12 +263,16 @@
         wv = [[row(v, l) for v in up] for l in range(4)]
         total = [None] * 4
         for n in range(4):
+            line = [None] * 4
             for m in range(4):
                 g = gather_point(quads, bx + m, by + n)
                 for l in range(4):
                     h = wv[l][0] * g[l] + wv[l][1] * g[l + 1] + wv[l][2] * g[l + 2]
-                    h = h * (wx[l][m] * wy[l][n])
-                    total[l] = h if total[l] is None else total[l] + h
+                    h = h * wx[l][m]
+                    line[l] = h if line[l] is None else line[l] + h
+            for l in range(4):
+                h = line[l] * wy[l][n]
+                total[l] = h if total[l] is None else total[l] + h
         new_ref[block] = jnp.concatenate(total, axis=0).astype(jnp.bfloat16)
         return carry
 

time: 27.6 us -> 27.6 us (level)
  no operation moved by 1% of the time
where the time goes in v3:
time: 27.6 us; the launch traced here: 27.4 us
  Pallas kernels  23.6 us (86%)
  local copies, waits for them, and re-layouts  3.14 us (11%)
  between operations  0.67 us (2%)
    pallas_call x1, Pallas kernels, body(): pl.pallas_call(functools.partial(kernel, n_tile, n_lev, nblocks), out_sha...  23.6 us
    reshape x1, local copies, waits for them, and re-layouts, body(): wind_field.reshape(3 * n_level, nblocks, cells)  0.85 us
    unnamed x8, local copies, waits for them, and re-layouts  0.79 us
    reshape x1, local copies, waits for them, and re-layouts, body(): new.reshape(nblocks, n_level, n_tracer, cells)  0.71 us
    transpose x2, local copies, waits for them, and re-layouts, body(): jnp.transpose(disp[:, :3 * n_level], (1, 0, 2))  0.68 us

profile of v3, /device:TPU:9, one launch (start us, length us, event | category | flops | bytes accessed | tf_op | source)
XLA Modules:
  0.0 27.4 jit_solution(9920912476581877403)
XLA Ops:
  0.6 0.0 copy-start.3
  0.6 0.8 %copy.20 = bf16[12,16,128]{2,0,1:T(8,128)(2,1)S(1)} copy(bf16[12,16,128]{2,1,0:T(8,128)(2,1)} %bitcast.25) | data formatting | bytes 98304 | tf_op jit(solution)/shard_map/reshape | solution.py:289
  1.5 0.0 copy-done.3
  1.6 0.0 copy-start
  1.6 0.0 copy-start.1
  1.6 0.0 copy-start.2
  1.6 0.1 copy.19
  1.7 0.7 %copy-done = s32[4,2,16,128]{3,2,1,0:T(8,128)S(1)} copy-done((s32[4,2,16,128]{3,2,1,0:T(8,128)S(1)}, s32[4,2,16,128]{3,2,1,0:T(8,128)}, u32[]{:S(2)}) %copy-start) | copy-done | bytes 65560
  2.4 0.0 copy-done.1
  2.4 0.0 copy-done.2
  2.4 23.6 %shard_map.68 = (bf16[16,32,128]{2,1,0:T(8,128)(2,1)S(1)}, f32[16,16,128]{2,1,0:T(8,128)S(1)}) custom-call(s32[4,2,16]{2,1,0:T(2,128)S(1)} %bitcast.19, s32[4,2,16]{2,1,0:T(2,128)S(1)} %bitcast.20, s32[4,2,16,128]{3,2,1,0:T(8,128)S(1)} %copy-done, bf16[16,16,128]{2,1,0:T(8,128)(2,1)S(1)} %pad.4.wind_ref, bf16[16,32,128]{2,1,0:T(8,128)(2,1)S(1)} %bitcast.17), custom_call_target="tpu_custom_call" | custom-call | tf_op jit(solution)/shard_map/pallas_call | solution.py:296
  26.0 0.7 %copy.18 = bf16[16,4,8,128]{3,0,1,2:T(8,128)(2,1)} copy(bf16[16,4,8,128]{3,2,1,0:T(8,128)(2,1)S(1)} %bitcast.18) | data formatting | bytes 262144 | tf_op jit(solution)/shard_map/reshape | solution.py:320
  26.7 0.7 %copy.14 = f32[12,16,128]{2,1,0:T(8,128)} copy(f32[12,16,128]{2,0,1:T(8,128)S(1)} %slice_bitcast_fusion) | data formatting | bytes 196608 | tf_op jit(solution)/shard_map/transpose | solution.py:321
  (2 shorter events, 0.0 us)
Async XLA Ops:
  0.6 0.9 %copy-start.3 = (bf16[8,4,16,128]{3,2,1,0:T(8,128)(2,1)S(1)}, bf16[8,4,16,128]{3,2,1,0:T(8,128)(2,1)}, u32[]{:S(2)}) copy-start(bf16[8,4,16,128]{3,2,1,0:T(8,128)(2,1)} %param.5) | copy-start | bytes 393220
  1.6 0.8 %copy-start = (s32[4,2,16,128]{3,2,1,0:T(8,128)S(1)}, s32[4,2,16,128]{3,2,1,0:T(8,128)}, u32[]{:S(2)}) copy-start(s32[4,2,16,128]{3,2,1,0:T(8,128)} %base_hbm.1) | copy-start | bytes 196612
  1.6 0.8 %copy-start.1 = (s32[4,16,2]{1,2,0:T(2,128)S(1)}, s32[4,16,2]{1,2,0:T(2,128)}, u32[]{:S(2)}) copy-start(s32[4,16,2]{1,2,0:T(2,128)} %param.7) | copy-start | bytes 1540
  1.6 0.8 %copy-start.2 = (s32[4,16,2]{1,2,0:T(2,128)S(1)}, s32[4,16,2]{1,2,0:T(2,128)}, u32[]{:S(2)}) copy-start(s32[4,16,2]{1,2,0:T(2,128)} %param.9) | copy-start | bytes 1540

commit v4 on v2

--- a/solution.py
+++ b/solution.py
@@ -229,8 +229,10 @@
     drain_recv(wind_relays)
     ahead = 3 * nblocks // 4
     lax.fori_loop(0, ahead, wind_step, 0, unroll=4)
-    drain_recv(tracer_copies)
-    start(tracer_relays)
+    drain_recv(tracer_copies[:2])
+    start(tracer_relays[:2])
+    drain_recv(tracer_copies[2:])
+    start(tracer_relays[2:])
     lax.fori_loop(ahead, nblocks, wind_step, 0, unroll=4)
     drain_recv(tracer_relays)
 

time: 27.6 us -> 27.5 us (level)
  no operation moved by 1% of the time
where the time goes in v4:
time: 27.5 us; the launch traced here: 27.4 us
  Pallas kernels  23.5 us (85%)
  local copies, waits for them, and re-layouts  3.14 us (11%)
  between operations  0.67 us (2%)
    pallas_call x1, Pallas kernels, body(): pl.pallas_call(functools.partial(kernel, n_tile, n_lev, nblocks), out_sha...  23.5 us
    reshape x1, local copies, waits for them, and re-layouts, body(): wind_field.reshape(3 * n_level, nblocks, cells)  0.85 us
    unnamed x8, local copies, waits for them, and re-layouts  0.79 us
    reshape x1, local copies, waits for them, and re-layouts, body(): new.reshape(nblocks, n_level, n_tracer, cells)  0.71 us
    transpose x2, local copies, waits for them, and re-layouts, body(): jnp.transpose(disp[:, :3 * n_level], (1, 0, 2))  0.68 us

profile of v4, /device:TPU:9, one launch (start us, length us, event | category | flops | bytes accessed | tf_op | source)
XLA Modules:
  0.0 27.4 jit_solution(2356648336567683749)
XLA Ops:
  0.6 0.0 copy-start.3
  0.6 0.8 %copy.20 = bf16[12,16,128]{2,0,1:T(8,128)(2,1)S(1)} copy(bf16[12,16,128]{2,1,0:T(8,128)(2,1)} %bitcast.25) | data formatting | bytes 98304 | tf_op jit(solution)/shard_map/reshape | solution.py:287
  1.5 0.0 copy-done.3
  1.6 0.0 copy-start
  1.6 0.0 copy-start.1
  1.6 0.0 copy-start.2
  1.6 0.1 copy.19
  1.7 0.7 %copy-done = s32[4,2,16,128]{3,2,1,0:T(8,128)S(1)} copy-done((s32[4,2,16,128]{3,2,1,0:T(8,128)S(1)}, s32[4,2,16,128]{3,2,1,0:T(8,128)}, u32[]{:S(2)}) %copy-start) | copy-done | bytes 65560
  2.4 0.0 copy-done.1
  2.4 0.0 copy-done.2
  2.4 23.5 %shard_map.68 = (bf16[16,32,128]{2,1,0:T(8,128)(2,1)S(1)}, f32[16,16,128]{2,1,0:T(8,128)S(1)}) custom-call(s32[4,2,16]{2,1,0:T(2,128)S(1)} %bitcast.19, s32[4,2,16]{2,1,0:T(2,128)S(1)} %bitcast.20, s32[4,2,16,128]{3,2,1,0:T(8,128)S(1)} %copy-done, bf16[16,16,128]{2,1,0:T(8,128)(2,1)S(1)} %pad.4.wind_ref, bf16[16,32,128]{2,1,0:T(8,128)(2,1)S(1)} %bitcast.17), custom_call_target="tpu_custom_call" | custom-call | tf_op jit(solution)/shard_map/pallas_call | solution.py:294
  26.0 0.7 %copy.18 = bf16[16,4,8,128]{3,0,1,2:T(8,128)(2,1)} copy(bf16[16,4,8,128]{3,2,1,0:T(8,128)(2,1)S(1)} %bitcast.18) | data formatting | bytes 262144 | tf_op jit(solution)/shard_map/reshape | solution.py:318
  26.7 0.7 %copy.14 = f32[12,16,128]{2,1,0:T(8,128)} copy(f32[12,16,128]{2,0,1:T(8,128)S(1)} %slice_bitcast_fusion) | data formatting | bytes 196608 | tf_op jit(solution)/shard_map/transpose | solution.py:319
  (2 shorter events, 0.0 us)
Async XLA Ops:
  0.6 0.9 %copy-start.3 = (bf16[8,4,16,128]{3,2,1,0:T(8,128)(2,1)S(1)}, bf16[8,4,16,128]{3,2,1,0:T(8,128)(2,1)}, u32[]{:S(2)}) copy-start(bf16[8,4,16,128]{3,2,1,0:T(8,128)(2,1)} %param.5) | copy-start | bytes 393220
  1.6 0.8 %copy-start = (s32[4,2,16,128]{3,2,1,0:T(8,128)S(1)}, s32[4,2,16,128]{3,2,1,0:T(8,128)}, u32[]{:S(2)}) copy-start(s32[4,2,16,128]{3,2,1,0:T(8,128)} %base_hbm.1) | copy-start | bytes 196612
  1.6 0.8 %copy-start.1 = (s32[4,16,2]{1,2,0:T(2,128)S(1)}, s32[4,16,2]{1,2,0:T(2,128)}, u32[]{:S(2)}) copy-start(s32[4,16,2]{1,2,0:T(2,128)} %param.7) | copy-start | bytes 1540
  1.6 0.8 %copy-start.2 = (s32[4,16,2]{1,2,0:T(2,128)S(1)}, s32[4,16,2]{1,2,0:T(2,128)}, u32[]{:S(2)}) copy-start(s32[4,16,2]{1,2,0:T(2,128)} %param.9) | copy-start | bytes 1540
